TPU v7x, 32 devices: a whole 2x2x4 slice. The times are simulated.
32 devices in a mesh: grp: 2 (over x), ao: 16 (over z, y, core).
Axes of the slice: x: 2, y: 2, z: 4, core: 2. Of those that a mesh axis runs over, the one named last changes fastest.
Arguments:
- chol_tiles: bfloat16 [32, 64, 128, 128], P(('grp', 'ao')), parts along dimension 0, may hold values from -6 to 6
- orbitals: bfloat16 [8192, 440], P('grp'), parts along dimension 0, may hold values from -0.29882812 to 0.29882812
- rdm_two: bfloat16 [3200, 1600], P('grp'), parts along dimension 0, may hold values from -0.0014648438 to 0.0014648438
- tile_row: int32 [32], P('grp'), parts along dimension 0, may hold values from 0 to 31
- tile_col: int32 [32], P('grp'), parts along dimension 0, may hold values from 0 to 31
- tile_live: int32 [32], P('grp'), parts along dimension 0, may hold values 0 or 1
Outputs:
- b_vectors: bfloat16 [128, 40, 440], P(('grp', 'ao')), parts along dimension 0
- q_matrix: float32 [880, 40], P('grp'), parts along dimension 0
There are 2 independent parts, one for each index of `grp`. A program takes and returns all parts, laid end to end along the dimension named above; each array names one. Nothing has to cross between parts.
All inputs are finite; a program needn't handle non-finite values.
Results may differ from a plain program's by a relative error of at most 0.0064.
Values may be sent and summed in bfloat16 or wider, within the bound.
A program may use at most 128 MiB of HBM per device.

v0:
```python
import jax
import jax.numpy as jnp
from jax import lax
from jax.sharding import PartitionSpec as P

TILE = 128
ACT = 40


def half_transform(tiles, cols_coef, live):
    half = jnp.einsum("svmn,sna->vsam", tiles, cols_coef, preferred_element_type=jnp.float32)
    return (half * live.astype(jnp.float32)[None, :, None, None]).astype(jnp.bfloat16)


def on_device(chol_tiles, orbitals, rdm_two, tile_row, tile_col, tile_live):
    nao = orbitals.shape[0]
    norb = orbitals.shape[1]
    ntiles = nao // TILE
    columns = jnp.arange(ntiles, dtype=jnp.int32)
    coef_tiles = orbitals.reshape(ntiles, TILE, norb)
    onehot_rows = (tile_row[:, None] == columns[None, :]).astype(jnp.bfloat16)
    onehot_cols = (tile_col[:, None] == columns[None, :]).astype(jnp.bfloat16)
    rows_coef = jnp.dot(
        onehot_rows, coef_tiles.reshape(ntiles, TILE * norb), preferred_element_type=jnp.float32
    )
    rows_coef = rows_coef.astype(jnp.bfloat16).reshape(-1, TILE, norb)
    active_tiles = coef_tiles[:, :, :ACT].reshape(ntiles, TILE * ACT)
    cols_coef = jnp.dot(onehot_cols, active_tiles, preferred_element_type=jnp.float32)
    cols_coef = cols_coef.astype(jnp.bfloat16).reshape(-1, TILE, ACT)
    arrived = lax.all_to_all(chol_tiles, "ao", split_axis=1, concat_axis=0, tiled=True)
    received = half_transform(arrived, cols_coef, tile_live)
    b_vectors = jnp.einsum(
        "vsam,smp->vap", received, rows_coef, preferred_element_type=jnp.float32
    ).astype(jnp.bfloat16)
    vec_here = b_vectors.shape[0]
    flat = b_vectors[:, :, :ACT].reshape(vec_here, ACT * ACT)
    zeta = jnp.dot(flat, rdm_two, preferred_element_type=jnp.float32).reshape(vec_here, ACT, ACT)
    q_local = jnp.einsum(
        "vup,vtu->pt", b_vectors.astype(jnp.float32), zeta, precision=lax.Precision.HIGHEST
    )
    q_matrix = lax.psum(q_local, "ao")
    return (b_vectors, q_matrix)


def solution(mesh):
    return jax.shard_map(
        on_device,
        mesh=mesh,
        in_specs=(
            P(("grp", "ao"), None, None, None),
            P("grp", None),
            P("grp", None),
            P("grp"),
            P("grp"),
            P("grp"),
        ),
        out_specs=(P(("grp", "ao"), None, None), P("grp", None)),
        check_vma=False,
    )
```

profile of v0, /device:TPU:0, one launch (start us, length us, event | category | flops | bytes accessed | tf_op | source)
XLA Modules:
  0.0 165.7 jit_solution(1449210334808666304)
XLA Ops:
  7.2 7.4 %all-to-all-start = ((bf16[1,64,128,128]{3,2,0,1:T(8,128)(2,1)}), bf16[1,64,128,128]{3,2,0,1:T(8,128)(2,1)}, u32[]{:S(2)}, u32[]{:S(2)}) async-start(bf16[1,64,128,128]{3,2,0,1:T(8,128)(2,1)} %bitcast.39), calls=%async_computation | async-start | bytes 4194304 | tf_op jit(solution)/shard_map/all_to_all | solution.py:30
  14.6 0.0 all-reduce.2.cloned.1.call-start
  14.7 6.4 %copy.31 = bf16[4096,440]{1,0:T(8,128)(2,1)} copy(bf16[4096,440]{0,1:T(8,128)(2,1)} %param.7) | data formatting | bytes 7208960 | tf_op jit(solution)/shard_map/reshape | solution.py:20
  21.1 0.0 copy-start.2
  21.1 8.4 %reshape_reshape.3 = bf16[32,56320]{1,0:T(8,128)(2,1)} reshape(bf16[4096,440]{1,0:T(8,128)(2,1)} %copy.31) | data formatting | bytes 7208960 | tf_op jit(solution)/shard_map/reshape;reshape | solution.py:24
  29.5 0.0 copy-done.2
  29.5 2.7 %convolution_convert_fusion = bf16[16,56320]{1,0:T(8,128)(2,1)S(1)} fusion(bf16[32,56320]{1,0:T(8,128)(2,1)} %reshape_reshape.3, s32[16]{0:T(128)S(1)} %copy-done.2), kind=kOutput, calls=%fused_computation | convolution fusion | flops 58573312 | bytes 5406784 | tf_op jit(solution)/shard_map/dot_general | solution.py:23
  32.2 5.9 %reshape.30 = bf16[16,128,440]{2,1,0:T(8,128)(2,1)} reshape(bf16[16,56320]{1,0:T(8,128)(2,1)S(1)} %convolution_convert_fusion) | data formatting | bytes 3604480 | tf_op jit(solution)/shard_map/reshape | solution.py:26
  38.1 0.0 copy-start.3
  38.1 0.0 copy-start.4
  38.1 1.3 slice.8
  39.4 1.9 %reshape.28 = bf16[32,5120]{1,0:T(8,128)(2,1)S(1)} reshape(bf16[32,128,40]{2,1,0:T(8,128)(2,1)S(1)} %slice.8) | data formatting | bytes 655360 | tf_op jit(solution)/shard_map/reshape | solution.py:27
  41.4 0.0 copy-done.3
  41.4 0.2 convolution_convert_fusion.1
  41.6 0.9 reshape.29
  42.5 0.0 copy-done.4
  42.6 0.0 copy-start
  42.6 9.4 %copy.26 = bf16[1600,1600]{0,1:T(8,128)(2,1)} copy(bf16[1600,1600]{1,0:T(8,128)(2,1)} %param.8) | data formatting | bytes 10240000 | tf_op args[2]
  52.0 3.8 %all-to-all-done = bf16[1,64,128,128]{3,2,0,1:T(8,128)(2,1)} async-done(((bf16[1,64,128,128]{3,2,0,1:T(8,128)(2,1)}), bf16[1,64,128,128]{3,2,0,1:T(8,128)(2,1)}, u32[]{:S(2)}, u32[]{:S(2)}) %all-to-all-start) | async-done | bytes 2097184 | tf_op jit(solution)/shard_map/all_to_all | solution.py:30
  55.8 0.0 copy-done
  55.8 2.8 %fusion.20 = bf16[4,40,440]{2,1,0:T(8,128)(2,1)S(1)} fusion(bf16[16,128,440]{2,1,0:T(8,128)(2,1)S(1)} %copy-done, bf16[16,4,128,128]{3,2,1,0:T(8,128)(2,1)} %bitcast.3, f32[16]{0:T(128)S(1)} %convert_element_type.22, bf16[16,128,40]{2,1,0:T(8,128)(2,1)S(1)} %reshape.29), kind=kOutput, calls=%fused_computation.10 | convolution fusion | flops 372970240 | bytes 4204096 | tf_op jit(solution)/shard_map/vsam,smp->vap/dot_general | solution.py:32
  58.6 0.0 copy-start.1
  58.6 0.1 reshape.35
  58.7 5.7 %fusion.31 = f32[4,40,40]{2,0,1:T(4,128)S(1)} fusion(bf16[4,1600,1]{1,0,2:T(4,128)(2,1)S(1)} %reshape.35, bf16[40,40,1600]{2,1,0:T(8,128)(2,1)} %bitcast.37), kind=kOutput, calls=%fused_computation.19 | convolution fusion | flops 20480000 | bytes 5158400 | tf_op jit(solution)/shard_map/dot_general | solution.py:37
  64.4 0.0 copy-done.1
  64.4 0.9 convolution_bitcast_fusion
  65.4 0.0 all-reduce.2.cloned.1.call-update
  65.4 91.9 %all-reduce.2.cloned.1.call-done = f32[440,40]{0,1:T(8,128)} async-done(((f32[440,40]{0,1:T(8,128)}), f32[440,40]{0,1:T(8,128)}) %all-reduce.2.cloned.1.call-update) | async-done | bytes 70416 | tf_op jit(solution)/shard_map/psum | solution.py:41
  157.3 1.5 copy.51
  (2 shorter events, 0.0 us)
Async XLA Ops:
  7.2 48.6 %all-to-all-start = ((bf16[1,64,128,128]{3,2,0,1:T(8,128)(2,1)}), bf16[1,64,128,128]{3,2,0,1:T(8,128)(2,1)}, u32[]{:S(2)}, u32[]{:S(2)}) async-start(bf16[1,64,128,128]{3,2,0,1:T(8,128)(2,1)} %bitcast.39), calls=%async_computation | async-start | bytes 4194304 | tf_op jit(solution)/shard_map/all_to_all | solution.py:30
  14.6 142.7 %all-reduce.2.cloned.1.call-start = ((), (), s32[]{:S(2)}) async-start(), calls=%async_computation.1 | async-start | bytes 163840 | tf_op jit(solution)/shard_map/psum | solution.py:41
  21.1 8.4 %copy-start.2 = (s32[16]{0:T(128)S(1)}, s32[16]{0:T(128)}, u32[]{:S(2)}) copy-start(s32[16]{0:T(128)} %param.9) | copy-start | bytes 196
  38.1 3.3 %copy-start.3 = (s32[16]{0:T(128)S(1)}, s32[16]{0:T(128)}, u32[]{:S(2)}) copy-start(s32[16]{0:T(128)} %param.10) | copy-start | bytes 196
  38.1 4.4 %copy-start.4 = (s32[16]{0:T(128)S(1)}, s32[16]{0:T(128)}, u32[]{:S(2)}) copy-start(s32[16]{0:T(128)} %param.11) | copy-start | bytes 196
  42.6 13.2 %copy-start = (bf16[16,128,440]{2,1,0:T(8,128)(2,1)S(1)}, bf16[16,128,440]{2,1,0:T(8,128)(2,1)}, u32[]{:S(2)}) copy-start(bf16[16,128,440]{2,1,0:T(8,128)(2,1)} %reshape.30) | copy-start | bytes 5406724
  58.6 5.8 %copy-start.1 = (bf16[4,40,440]{2,1,0:T(8,128)(2,1)}, bf16[4,40,440]{2,1,0:T(8,128)(2,1)S(1)}, u32[]{:S(2)}) copy-start(bf16[4,40,440]{2,1,0:T(8,128)(2,1)S(1)} %fusion.20) | copy-start | bytes 422404
Sparse Core Ops, SparseCore 0:
  65.5 91.7 all-reduce.1
where the time goes:
time: 167 us; the launch traced here: 166 us
  waiting for transfers between devices  95.7 us (57%)
  local copies, waits for them, and re-layouts  36 us (22%)
  between operations  14.1 us (8%)
  matrix products  12.4 us (7%)
  starting transfers between devices  7.49 us (4%)
    psum x1, waiting for transfers between devices, on_device(): q_matrix = lax.psum(q_local, 'ao')  91.9 us
    unnamed x12, local copies, waits for them, and re-layouts  11 us
    another operation x1, local copies, waits for them, and re-layouts, on_device(): coef_tiles.reshape(ntiles, TILE * norb)  8.43 us
    all_to_all x1, starting transfers between devices, on_device(): lax.all_to_all(chol_tiles, 'ao', split_axis=1, concat_axis=0, tiled=True)  7.45 us
    reshape x1, local copies, waits for them, and re-layouts, on_device(): coef_tiles = orbitals.reshape(ntiles, TILE, norb)  6.41 us
    reshape x1, local copies, waits for them, and re-layouts, on_device(): rows_coef = rows_coef.astype(jnp.bfloat16).reshape(-1, TILE, norb)  5.89 us
    dot_general x1, matrix products, on_device(): jnp.dot(flat, rdm_two, preferred_element_type=jnp.float32)  5.69 us
    all_to_all x1, waiting for transfers between devices, on_device(): lax.all_to_all(chol_tiles, 'ao', split_axis=1, concat_axis=0, tiled=True)  3.76 us
  transfers between devices with their start and end apart: 2, of which 2 were waited for; matrix products, arithmetic and copies ran while one was open for 23% of the time, Pallas kernels for 0%

commit v1 on v0

v1 whole, which is shorter than its diff:
```python
import jax
import jax.numpy as jnp
from jax import lax
from jax.sharding import PartitionSpec as P

TILE = 128
ACT = 40


def on_device(chol_tiles, orbitals, rdm_two, tile_row, tile_col, tile_live):
    nao = orbitals.shape[0]
    norb = orbitals.shape[1]
    ntiles = nao // TILE
    slots_here = chol_tiles.shape[0]
    coef_tiles = orbitals.reshape(ntiles, TILE, norb)
    first = lax.axis_index("ao") * slots_here
    col_here = lax.dynamic_slice_in_dim(tile_col, first, slots_here)
    live_here = lax.dynamic_slice_in_dim(tile_live, first, slots_here)
    cols_coef = coef_tiles[col_here][:, :, :ACT]
    rows_coef = coef_tiles[tile_row]
    half = jnp.einsum("svmn,sna->vsam", chol_tiles, cols_coef, preferred_element_type=jnp.float32)
    half = (half * live_here.astype(jnp.float32)[None, :, None, None]).astype(jnp.bfloat16)
    received = lax.all_to_all(half, "ao", split_axis=0, concat_axis=1, tiled=True)
    b_vectors = jnp.einsum(
        "vsam,smp->vap", received, rows_coef, preferred_element_type=jnp.float32
    ).astype(jnp.bfloat16)
    vec_here = b_vectors.shape[0]
    flat = b_vectors[:, :, :ACT].reshape(vec_here, ACT * ACT)
    zeta = jnp.dot(flat, rdm_two, preferred_element_type=jnp.float32).reshape(vec_here, ACT, ACT)
    q_local = jnp.einsum(
        "vup,vtu->pt", b_vectors.astype(jnp.float32), zeta, precision=lax.Precision.HIGHEST
    )
    q_matrix = lax.psum(q_local, "ao")
    return (b_vectors, q_matrix)


def solution(mesh):
    return jax.shard_map(
        on_device,
        mesh=mesh,
        in_specs=(
            P(("grp", "ao"), None, None, None),
            P("grp", None),
            P("grp", None),
            P("grp"),
            P("grp"),
            P("grp"),
        ),
        out_specs=(P(("grp", "ao"), None, None), P("grp", None)),
        check_vma=False,
    )
```

time: 167 us -> 146 us (0.87)
  local copies, waits for them, and re-layouts: 36 us -> 21.4 us
  waiting for transfers between devices: 95.7 us -> 88.6 us
  between operations: 14.1 us -> 16.8 us
    reshape x3 -> x0, local copies, waits for them, and re-layouts: 8.72 us -> none  [the longest x1 5.89 us: on_device(): rows_coef = rows_coef.astype(jnp.bfloat16).reshape(-1, TILE, norb)]
    another operation x1 -> x0, local copies, waits for them, and re-layouts: 8.43 us -> none  [on_device(): coef_tiles.reshape(ntiles, TILE * norb)]
    psum x1, waiting for transfers between devices: 91.9 us -> 85.5 us  [on_device(): q_matrix = lax.psum(q_local, 'ao')]
    gather x0 -> x1, local copies, waits for them, and re-layouts: none -> 4.06 us  [on_device(): rows_coef = coef_tiles[tile_row]]
    reshape x1, local copies, waits for them, and re-layouts: 6.41 us -> 2.64 us  [on_device(): coef_tiles = orbitals.reshape(ntiles, TILE, norb)]
    dynamic_slice x0 -> x2, local copies, waits for them, and re-layouts: none -> 2.63 us  [the longest x1 1.39 us: on_device(): live_here = lax.dynamic_slice_in_dim(tile_live, first, slots_here)]
    unnamed x12 -> x10, local copies, waits for them, and re-layouts: 11 us -> 12 us
  transfers between devices with their start and end apart: 2 -> 2, of which waited for: 2 -> 2; matrix products, arithmetic and copies ran while one was open for 23% -> 9% of each run, Pallas kernels for 0% -> 0%
where the time goes in v1:
time: 146 us; the launch traced here: 145 us
  waiting for transfers between devices  88.6 us (61%)
  local copies, waits for them, and re-layouts  21.4 us (15%)
  between operations  16.8 us (12%)
  matrix products  10.9 us (7%)
  starting transfers between devices  7.43 us (5%)
    psum x1, waiting for transfers between devices, on_device(): q_matrix = lax.psum(q_local, 'ao')  85.5 us
    unnamed x10, local copies, waits for them, and re-layouts  12 us
    all_to_all x1, starting transfers between devices, on_device(): lax.all_to_all(half, 'ao', split_axis=0, concat_axis=1, tiled=True)  7.39 us
    dot_general x1, matrix products, on_device(): jnp.dot(flat, rdm_two, preferred_element_type=jnp.float32)  5.69 us
    gather x1, local copies, waits for them, and re-layouts, on_device(): rows_coef = coef_tiles[tile_row]  4.06 us
    all_to_all x1, waiting for transfers between devices, on_device(): lax.all_to_all(half, 'ao', split_axis=0, concat_axis=1, tiled=True)  3.05 us
  transfers between devices with their start and end apart: 2, of which 2 were waited for; matrix products, arithmetic and copies ran while one was open for 9% of the time, Pallas kernels for 0%

profile of v1, /device:TPU:0, one launch (start us, length us, event | category | flops | bytes accessed | tf_op | source)
XLA Modules:
  0.0 145.1 jit_solution(9179091006515885937)
XLA Ops:
  7.2 0.0 copy-start
  7.2 1.4 dynamic_slice.7
  9.2 1.2 dynamic_slice.6
  11.8 2.6 %copy_bitcast_fusion = bf16[32,128,440]{1,2,0:T(8,128)(2,1)S(1)} fusion(bf16[4096,440]{0,1:T(8,128)(2,1)} %param.7), kind=kLoop, calls=%fused_computation.1 | loop fusion | bytes 7208960 | tf_op jit(solution)/shard_map/reshape | solution.py:15
  14.4 0.0 copy-start.1
  14.4 0.0 copy-start.3
  15.2 1.0 copy-done.1
  16.2 0.0 copy-done
  16.2 2.1 %fusion.10 = bf16[64,1,40,128]{3,2,1,0:T(8,128)(2,1)} fusion(bf16[1,64,128,128]{3,2,1,0:T(8,128)(2,1)S(1)} %copy-done, f32[]{:T(128)} %bitcast.4, bf16[32,128,440]{1,2,0:T(8,128)(2,1)S(1)} %copy_bitcast_fusion, s32[]{:T(128)} %bitcast), kind=kOutput, calls=%fused_computation.8 | convolution fusion | flops 84541440 | bytes 2762760 | tf_op jit(solution)/shard_map/svmn,sna->vsam/dot_general | solution.py:21
  18.3 7.4 %all-to-all-start = ((bf16[64,1,40,128]{3,2,1,0:T(8,128)(2,1)}), bf16[64,1,40,128]{3,2,1,0:T(8,128)(2,1)S(1)}, u32[]{:S(2)}, u32[]{:S(2)}) async-start(bf16[64,1,40,128]{3,2,1,0:T(8,128)(2,1)} %fusion.10), calls=%async_computation | async-start | bytes 1310720 | tf_op jit(solution)/shard_map/all_to_all | solution.py:23
  25.7 0.0 all-reduce.2.cloned.1.call-start
  25.8 0.0 copy-done.3
  25.8 4.1 %gather_fusion = bf16[16,128,440]{1,2,0:T(8,128)(2,1)} fusion(bf16[32,128,440]{1,2,0:T(8,128)(2,1)} %copy-done.1, s32[1024]{0:T(1024)S(1)} %pad_clamp_fusion), kind=kCustom, calls=%fused_computation | custom fusion | bytes 3604544 | tf_op jit(solution)/shard_map/gather | solution.py:20
  29.9 9.4 %copy.20 = bf16[1600,1600]{0,1:T(8,128)(2,1)} copy(bf16[1600,1600]{1,0:T(8,128)(2,1)} %param.8) | data formatting | bytes 10240000 | tf_op args[2]
  39.3 3.0 %all-to-all-done = bf16[64,1,40,128]{3,2,1,0:T(8,128)(2,1)S(1)} async-done(((bf16[64,1,40,128]{3,2,1,0:T(8,128)(2,1)}), bf16[64,1,40,128]{3,2,1,0:T(8,128)(2,1)S(1)}, u32[]{:S(2)}, u32[]{:S(2)}) %all-to-all-start) | async-done | bytes 655392 | tf_op jit(solution)/shard_map/all_to_all | solution.py:23
  42.3 2.2 %fusion.16 = bf16[4,40,440]{2,1,0:T(8,128)(2,1)S(1)} fusion(bf16[4,16,40,128]{3,2,0,1:T(8,128)(2,1)S(1)} %bitcast.54, bf16[16,128,440]{1,2,0:T(8,128)(2,1)} %gather_fusion), kind=kOutput, calls=%fused_computation.10 | convolution fusion | flops 288428800 | bytes 2598400 | tf_op jit(solution)/shard_map/vsam,smp->vap/dot_general | solution.py:24
  44.5 0.0 copy-start.2
  44.5 0.1 reshape.63
  44.6 5.7 %fusion.21 = f32[4,40,40]{2,0,1:T(4,128)S(1)} fusion(bf16[4,1600,1]{1,0,2:T(4,128)(2,1)S(1)} %reshape.63, bf16[40,40,1600]{2,1,0:T(8,128)(2,1)} %bitcast.53), kind=kOutput, calls=%fused_computation.17 | convolution fusion | flops 20480000 | bytes 5158400 | tf_op jit(solution)/shard_map/dot_general | solution.py:29
  50.3 0.9 convolution_bitcast_fusion
  51.2 0.0 all-reduce.2.cloned.1.call-update
  51.3 85.5 %all-reduce.2.cloned.1.call-done = f32[440,40]{0,1:T(8,128)} async-done(((f32[440,40]{0,1:T(8,128)}), f32[440,40]{0,1:T(8,128)}) %all-reduce.2.cloned.1.call-update) | async-done | bytes 70416 | tf_op jit(solution)/shard_map/psum | solution.py:33
  136.8 1.5 %copy.28 = f32[440,40]{0,1:T(8,128)} copy(f32[440,40]{0,1:T(8,128)} %all-reduce.2.cloned.1.call-done) | data formatting | bytes 140800
  138.3 0.0 copy-done.2
  (3 shorter events, 0.0 us)
Async XLA Ops:
  7.2 9.0 %copy-start = (bf16[1,64,128,128]{3,2,1,0:T(8,128)(2,1)S(1)}, bf16[1,64,128,128]{3,2,1,0:T(8,128)(2,1)}, u32[]{:S(2)}) copy-start(bf16[1,64,128,128]{3,2,1,0:T(8,128)(2,1)} %param.6) | copy-start | bytes 6291460
  14.4 1.8 %copy-start.1 = (bf16[32,128,440]{1,2,0:T(8,128)(2,1)}, bf16[32,128,440]{1,2,0:T(8,128)(2,1)S(1)}, u32[]{:S(2)}) copy-start(bf16[32,128,440]{1,2,0:T(8,128)(2,1)S(1)} %copy_bitcast_fusion) | copy-start | bytes 10813444
  14.4 11.4 %copy-start.3 = (s32[16]{0:T(128)S(1)}, s32[16]{0:T(128)}, u32[]{:S(2)}) copy-start(s32[16]{0:T(128)} %param.9) | copy-start | bytes 196
  18.3 24.0 %all-to-all-start = ((bf16[64,1,40,128]{3,2,1,0:T(8,128)(2,1)}), bf16[64,1,40,128]{3,2,1,0:T(8,128)(2,1)S(1)}, u32[]{:S(2)}, u32[]{:S(2)}) async-start(bf16[64,1,40,128]{3,2,1,0:T(8,128)(2,1)} %fusion.10), calls=%async_computation | async-start | bytes 1310720 | tf_op jit(solution)/shard_map/all_to_all | solution.py:23
  25.7 111.0 %all-reduce.2.cloned.1.call-start = ((), (), s32[]{:S(2)}) async-start(), calls=%async_computation.1 | async-start | bytes 163840 | tf_op jit(solution)/shard_map/psum | solution.py:33
  44.5 93.8 %copy-start.2 = (bf16[4,40,440]{2,1,0:T(8,128)(2,1)}, bf16[4,40,440]{2,1,0:T(8,128)(2,1)S(1)}, u32[]{:S(2)}) copy-start(bf16[4,40,440]{2,1,0:T(8,128)(2,1)S(1)} %fusion.16) | copy-start | bytes 422404
Sparse Core Ops, SparseCore 0:
  51.4 85.3 all-reduce.1

commit v2 on v1

v2 whole, which is shorter than its diff:
```python
import functools

import jax
import jax.numpy as jnp
from jax import lax
from jax.experimental import pallas as pl
from jax.experimental.pallas import tpu as pltpu
from jax.sharding import PartitionSpec as P

TILE = 128
ACT = 40
MESH = pl.DeviceIdType.MESH
F32 = jnp.float32
BF16 = jnp.bfloat16
NT_DIMS = (((1,), (1,)), ((), ()))


def kernel(
    n, vec, norb, per, owners,
    row_ref, col_ref, live_ref, chol_hbm, orb_hbm, rdm_hbm,
    b_ref, q_ref,
    chol, orb_act, orb, rdm, sent, got, acc, zeta_t, q_parts, q_got, q_sum, q_full,
    load_sem, send_sem, recv_sem, rs_send, rs_recv, ag_send, ag_recv,
):
    me = lax.axis_index("ao")
    rows = vec * ACT
    flat_len = ACT * ACT
    lane_blocks = -(-norb // 128)
    owner_dev = [(o * n) // owners for o in range(owners)]

    loads = [
        pltpu.make_async_copy(orb_hbm.at[:, :, pl.ds(0, TILE)], orb_act, load_sem.at[0]),
        pltpu.make_async_copy(chol_hbm.at[0], chol, load_sem.at[1]),
        pltpu.make_async_copy(orb_hbm, orb, load_sem.at[2]),
        pltpu.make_async_copy(rdm_hbm, rdm, load_sem.at[3]),
    ]
    for load in loads:
        load.start()

    barrier = pltpu.get_barrier_semaphore()

    def greet(d, carry):
        pl.semaphore_signal(
            barrier, inc=1, device_id={"ao": lax.rem(me + d, n)}, device_id_type=MESH
        )
        return carry

    lax.fori_loop(1, n, greet, 0)

    q_parts[...] = jnp.zeros_like(q_parts)
    acc[...] = jnp.zeros_like(acc)
    live = live_ref[me].astype(F32)
    loads[0].wait()
    cols = orb_act[col_ref[me]]
    cols_t = jnp.transpose(cols.astype(F32))[:ACT].astype(BF16)
    loads[1].wait()

    def half(dest):
        tiles = chol[pl.ds(dest * vec, vec)].reshape(vec * TILE, TILE)
        out = lax.dot_general(cols_t, tiles, NT_DIMS, preferred_element_type=F32) * live
        parts = [out[:, v * TILE : (v + 1) * TILE] for v in range(vec)]
        return jnp.concatenate(parts, axis=0).astype(BF16)

    def distance(i):
        off = (i + 1) // 2
        return n // 2 + off * (2 * ((i + 1) % 2) - 1)

    def slot_copy(there, mine):
        return pltpu.make_async_remote_copy(
            src_ref=sent.at[there],
            dst_ref=got.at[mine],
            send_sem=send_sem.at[there],
            recv_sem=recv_sem.at[mine],
            device_id={"ao": there},
            device_id_type=MESH,
        )

    far = lax.rem(me + n // 2, n)
    sent[far] = half(far)
    pl.semaphore_wait(barrier, n - 1)
    slot_copy(far, me).start()

    def send_step(i, carry):
        dest = lax.rem(me + distance(i), n)
        sent[dest] = half(dest)
        slot_copy(dest, me).start()
        return carry

    lax.fori_loop(1, n - 1, send_step, 0, unroll=n <= 16)

    own = half(me)
    column = lax.broadcasted_iota(jnp.int32, (1, flat_len), 1)
    lane_of = column - (column // ACT) * ACT
    pick = (lax.broadcasted_iota(jnp.int32, (TILE, flat_len), 0) == lane_of).astype(F32).astype(BF16)
    mask = lax.broadcasted_iota(jnp.int32, (ACT, flat_len), 0) == column // ACT
    loads[2].wait()

    def coef(slot):
        return orb[row_ref[slot]]

    acc[...] += jnp.dot(own, coef(me), preferred_element_type=F32)

    def take_step(j, carry):
        src = lax.rem(me + n - distance(n - 2 - j), n)
        pltpu.make_async_remote_copy(
            src_ref=sent.at[src],
            dst_ref=got.at[src],
            send_sem=send_sem.at[src],
            recv_sem=recv_sem.at[src],
            device_id={"ao": src},
            device_id_type=MESH,
        ).wait_recv()
        acc[...] += jnp.dot(got[src], coef(src), preferred_element_type=F32)
        return carry

    lax.fori_loop(0, n - 1, take_step, 0, unroll=n <= 16)

    b16 = acc[...].astype(BF16)
    b_ref[...] = b16
    spread = jnp.dot(b16[:, :TILE], pick, preferred_element_type=F32)
    flat = jnp.concatenate(
        [
            jnp.sum(jnp.where(mask, spread[v * ACT : (v + 1) * ACT], 0.0), axis=0, keepdims=True)
            for v in range(vec)
        ],
        axis=0,
    ).astype(BF16)
    loads[3].wait()
    zeta = jnp.dot(flat, rdm[...], preferred_element_type=F32)
    for t in range(ACT):
        zeta_t[t] = zeta[:, t * ACT : (t + 1) * ACT]
    b32 = b16.astype(F32)
    q_t = jnp.zeros((ACT, norb), F32)
    for v in range(vec):
        z = zeta_t[:, v, :]
        high = z.astype(BF16)
        low = (z - high.astype(F32)).astype(BF16)
        b_v = b32[v * ACT : (v + 1) * ACT].astype(BF16)
        q_t += jnp.dot(high, b_v, preferred_element_type=F32)
        q_t += jnp.dot(low, b_v, preferred_element_type=F32)

    def block_of(k):
        r, c = k // lane_blocks, k % lane_blocks
        return r * 8, c * 128, min(128, norb - c * 128)

    blocks = (ACT // 8) * lane_blocks
    for k in range(blocks):
        r, c, wide = block_of(k)
        q_parts[k // per, k % per, :, pl.ds(0, wide)] = q_t[r : r + 8, c : c + wide]

    def rs_copy(o):
        return pltpu.make_async_remote_copy(
            src_ref=q_parts.at[o],
            dst_ref=q_got.at[me],
            send_sem=rs_send.at[o],
            recv_sem=rs_recv.at[me],
            device_id={"ao": owner_dev[o]},
            device_id_type=MESH,
        )

    def ag_copy(o, dest):
        return pltpu.make_async_remote_copy(
            src_ref=q_sum,
            dst_ref=q_full.at[o],
            send_sem=ag_send.at[dest],
            recv_sem=ag_recv.at[o],
            device_id={"ao": dest},
            device_id_type=MESH,
        )

    for o in range(owners):
        @pl.when(me != owner_dev[o])
        def _():
            rs_copy(o).start()

    for o in range(owners):
        @pl.when(me == owner_dev[o])
        def _():
            q_sum[...] = q_parts[o]

            def add_step(d, carry):
                src = lax.rem(me + d, n)
                pltpu.make_async_remote_copy(
                    src_ref=q_parts.at[o],
                    dst_ref=q_got.at[src],
                    send_sem=rs_send.at[o],
                    recv_sem=rs_recv.at[src],
                    device_id={"ao": src},
                    device_id_type=MESH,
                ).wait_recv()
                q_sum[...] += q_got[src]
                return carry

            lax.fori_loop(1, n, add_step, 0)

            def spread_step(d, carry):
                ag_copy(o, lax.rem(me + d, n)).start()
                return carry

            lax.fori_loop(1, n, spread_step, 0)
            q_full[o] = q_sum[...]

    for o in range(owners):
        @pl.when(me != owner_dev[o])
        def _():
            ag_copy(o, owner_dev[o]).wait_recv()

    for k in range(blocks):
        r, c, wide = block_of(k)
        q_ref[pl.ds(r, 8), pl.ds(c, wide)] = q_full[k // per, k % per, :, pl.ds(0, wide)]

    def drain(d, carry):
        dest = lax.rem(me + d, n)
        slot_copy(dest, me).wait_send()
        return carry

    lax.fori_loop(1, n, drain, 0)
    for o in range(owners):
        @pl.when(me != owner_dev[o])
        def _():
            rs_copy(o).wait_send()

        @pl.when(me == owner_dev[o])
        def _():
            def done(d, carry):
                ag_copy(o, lax.rem(me + d, n)).wait_send()
                return carry

            lax.fori_loop(1, n, done, 0)


def solution(mesh):
    n = mesh.shape["ao"]

    def on_device(chol_tiles, orbitals, rdm_two, tile_row, tile_col, tile_live):
        nao, norb = orbitals.shape
        vec_all = chol_tiles.shape[1]
        vec = vec_all // n
        rows = vec * ACT
        blocks = (ACT // 8) * (-(-norb // 128))
        per = -(-blocks // n)
        owners = -(-blocks // per)
        b, q_t = pl.pallas_call(
            functools.partial(kernel, n, vec, norb, per, owners),
            out_shape=(
                jax.ShapeDtypeStruct((rows, norb), BF16),
                jax.ShapeDtypeStruct((ACT, norb), F32),
            ),
            in_specs=[pl.BlockSpec(memory_space=pltpu.SMEM)] * 3
            + [pl.BlockSpec(memory_space=pl.ANY)] * 3,
            out_specs=(
                pl.BlockSpec(memory_space=pltpu.VMEM),
                pl.BlockSpec(memory_space=pltpu.VMEM),
            ),
            scratch_shapes=[
                pltpu.VMEM((vec_all, TILE, TILE), BF16),
                pltpu.VMEM((nao // TILE, TILE, TILE), BF16),
                pltpu.VMEM((nao // TILE, TILE, norb), BF16),
                pltpu.VMEM(rdm_two.shape, BF16),
                pltpu.VMEM((n, rows, TILE), BF16),
                pltpu.VMEM((n, rows, TILE), BF16),
                pltpu.VMEM((rows, norb), F32),
                pltpu.VMEM((ACT, vec, ACT), F32),
                pltpu.VMEM((owners, per, 8, 128), F32),
                pltpu.VMEM((n, per, 8, 128), F32),
                pltpu.VMEM((per, 8, 128), F32),
                pltpu.VMEM((owners, per, 8, 128), F32),
                pltpu.SemaphoreType.DMA((4,)),
                pltpu.SemaphoreType.DMA((n,)),
                pltpu.SemaphoreType.DMA((n,)),
                pltpu.SemaphoreType.DMA((owners,)),
                pltpu.SemaphoreType.DMA((n,)),
                pltpu.SemaphoreType.DMA((n,)),
                pltpu.SemaphoreType.DMA((owners,)),
            ],
            compiler_params=pltpu.CompilerParams(
                collective_id=0, has_side_effects=True, vmem_limit_bytes=56 * 1024 * 1024
            ),
        )(
            tile_row, tile_col, tile_live, chol_tiles,
            orbitals.reshape(nao // TILE, TILE, norb), rdm_two,
        )
        return b.reshape(vec, ACT, norb), q_t.T

    return jax.shard_map(
        on_device,
        mesh=mesh,
        in_specs=(
            P(("grp", "ao"), None, None, None),
            P("grp", None),
            P("grp", None),
            P("grp"),
            P("grp"),
            P("grp"),
        ),
        out_specs=(P(("grp", "ao"), None, None), P("grp", None)),
        check_vma=False,
    )
```

time: 146 us -> 45.8 us (0.31)
  waiting for transfers between devices: 88.6 us -> 0 us
  Pallas kernels: 0 us -> 35.4 us
  between operations: 16.8 us -> 0.64 us
  local copies, waits for them, and re-layouts: 21.4 us -> 9.53 us
  matrix products: 10.9 us -> 0 us
  starting transfers between devices: 7.43 us -> 0 us
    psum x1 -> x0, waiting for transfers between devices: 85.5 us -> none  [on_device(): q_matrix = lax.psum(q_local, 'ao')]
    pallas_call x0 -> x1, Pallas kernels: none -> 35.4 us  [on_device(): pl.pallas_call(functools.partial(kernel, n, vec, norb, per, owners), out_...]
    dot_general x4 -> x0, matrix products: 10.9 us -> none  [the longest x1 5.69 us: on_device(): jnp.dot(flat, rdm_two, preferred_element_type=jnp.float32)]
    all_to_all x1 -> x0, starting transfers between devices: 7.39 us -> none  [on_device(): lax.all_to_all(half, 'ao', split_axis=0, concat_axis=1, tiled=True)]
    gather x1 -> x0, local copies, waits for them, and re-layouts: 4.06 us -> none  [on_device(): rows_coef = coef_tiles[tile_row]]
    all_to_all x1 -> x0, waiting for transfers between devices: 3.05 us -> none  [on_device(): lax.all_to_all(half, 'ao', split_axis=0, concat_axis=1, tiled=True)]
    reshape x2 -> x0, local copies, waits for them, and re-layouts: 2.75 us -> none  [the longest x1 2.64 us: on_device(): coef_tiles = orbitals.reshape(ntiles, TILE, norb)]
    dynamic_slice x2 -> x0, local copies, waits for them, and re-layouts: 2.63 us -> none  [the longest x1 1.39 us: on_device(): live_here = lax.dynamic_slice_in_dim(tile_live, first, slots_here)]
  transfers between devices with their start and end apart: 2 -> 0, of which waited for: 2 -> 0; matrix products, arithmetic and copies ran while one was open for 9% -> 0% of each run, Pallas kernels for 0% -> 0%
where the time goes in v2:
time: 45.8 us; the launch traced here: 45.5 us
  Pallas kernels  35.4 us (77%)
  local copies, waits for them, and re-layouts  9.53 us (21%)
  between operations  0.64 us (1%)
    pallas_call x1, Pallas kernels, on_device(): pl.pallas_call(functools.partial(kernel, n, vec, norb, per, owners), out_...  35.4 us
    unnamed x3, local copies, waits for them, and re-layouts  9.53 us

profile of v2, /device:TPU:0, one launch (start us, length us, event | category | flops | bytes accessed | tf_op | source)
XLA Modules:
  0.0 45.5 jit_solution(2807590600729360451)
XLA Ops:
  0.6 6.4 %copy.8 = bf16[4096,440]{1,0:T(8,128)(2,1)} copy(bf16[4096,440]{0,1:T(8,128)(2,1)} %param.7) | data formatting | bytes 7208960 | tf_op args[1]
  7.0 35.4 %shard_map.77 = (bf16[160,440]{1,0:T(8,128)(2,1)}, f32[40,440]{1,0:T(8,128)}) custom-call(s32[16]{0:T(128)} %row_ref.1, s32[16]{0:T(128)} %col_ref.1, s32[16]{0:T(128)} %live_ref.1, bf16[1,64,128,128]{3,2,1,0:T(8,128)(2,1)} %chol_hbm.1, bf16[32,128,440]{2,1,0:T(8,128)(2,1)} %bitcast.3, bf16[1600,1600]{1,0:T(8,128)(2,1)} %rdm_hbm.1), custom_call_target="tpu_custom_call" | custom-call | tf_op jit(solution)/shard_map/pallas_call | solution.py:243
  42.4 1.6 %copy.11 = bf16[4,40,440]{2,1,0:T(8,128)(2,1)} copy(bf16[4,40,440]{2,1,0:T(8,128)(2,1)} %bitcast.4) | data formatting | bytes 281600
  44.0 1.5 %copy.12 = f32[440,40]{0,1:T(8,128)} copy(f32[440,40]{0,1:T(8,128)} %bitcast.5) | data formatting | bytes 140800

commit v3 on v2

--- a/solution.py
+++ b/solution.py
@@ -9,6 +9,7 @@
 
 TILE = 128
 ACT = 40
+ACT_ROWS = 48
 MESH = pl.DeviceIdType.MESH
 F32 = jnp.float32
 BF16 = jnp.bfloat16
@@ -19,7 +20,7 @@
     n, vec, norb, per, owners,
     row_ref, col_ref, live_ref, chol_hbm, orb_hbm, rdm_hbm,
     b_ref, q_ref,
-    chol, orb_act, orb, rdm, sent, got, acc, zeta_t, q_parts, q_got, q_sum, q_full,
+    chol, act_wide, act, orb, rdm, sent, got, acc, zeta_t, q_parts, q_got, q_sum, q_full,
     load_sem, send_sem, recv_sem, rs_send, rs_recv, ag_send, ag_recv,
 ):
     me = lax.axis_index("ao")
@@ -29,13 +30,13 @@
     owner_dev = [(o * n) // owners for o in range(owners)]
 
     loads = [
-        pltpu.make_async_copy(orb_hbm.at[:, :, pl.ds(0, TILE)], orb_act, load_sem.at[0]),
+        pltpu.make_async_copy(orb_hbm.at[pl.ds(0, ACT_ROWS)], act_wide, load_sem.at[0]),
         pltpu.make_async_copy(chol_hbm.at[0], chol, load_sem.at[1]),
-        pltpu.make_async_copy(orb_hbm, orb, load_sem.at[2]),
-        pltpu.make_async_copy(rdm_hbm, rdm, load_sem.at[3]),
+        pltpu.make_async_copy(rdm_hbm, rdm, load_sem.at[2]),
     ]
-    for load in loads:
-        load.start()
+    loads[0].start()
+    loads[1].start()
+    ntiles = orb.shape[0]
 
     barrier = pltpu.get_barrier_semaphore()
 
@@ -48,16 +49,17 @@
     lax.fori_loop(1, n, greet, 0)
 
     q_parts[...] = jnp.zeros_like(q_parts)
-    acc[...] = jnp.zeros_like(acc)
     live = live_ref[me].astype(F32)
     loads[0].wait()
-    cols = orb_act[col_ref[me]]
-    cols_t = jnp.transpose(cols.astype(F32))[:ACT].astype(BF16)
+    for k in range(ntiles):
+        act[k] = act_wide[:, k * TILE : (k + 1) * TILE]
+    cols_t = act[col_ref[me]]
     loads[1].wait()
 
     def half(dest):
         tiles = chol[pl.ds(dest * vec, vec)].reshape(vec * TILE, TILE)
-        out = lax.dot_general(cols_t, tiles, NT_DIMS, preferred_element_type=F32) * live
+        out = lax.dot_general(cols_t, tiles, NT_DIMS, preferred_element_type=F32)
+        out = out[:ACT] * live
         parts = [out[:, v * TILE : (v + 1) * TILE] for v in range(vec)]
         return jnp.concatenate(parts, axis=0).astype(BF16)
 
@@ -79,6 +81,11 @@
     sent[far] = half(far)
     pl.semaphore_wait(barrier, n - 1)
     slot_copy(far, me).start()
+    for k in range(ntiles):
+        pltpu.make_async_copy(
+            orb_hbm.at[:, pl.ds(k * TILE, TILE)], orb.at[k], load_sem.at[3]
+        ).start()
+    loads[2].start()
 
     def send_step(i, carry):
         dest = lax.rem(me + distance(i), n)
@@ -93,12 +100,12 @@
     lane_of = column - (column // ACT) * ACT
     pick = (lax.broadcasted_iota(jnp.int32, (TILE, flat_len), 0) == lane_of).astype(F32).astype(BF16)
     mask = lax.broadcasted_iota(jnp.int32, (ACT, flat_len), 0) == column // ACT
-    loads[2].wait()
-
-    def coef(slot):
-        return orb[row_ref[slot]]
-
-    acc[...] += jnp.dot(own, coef(me), preferred_element_type=F32)
+    pltpu.make_async_copy(orb, orb, load_sem.at[3]).wait()
+
+    def second(block, slot):
+        return lax.dot_general(block, orb[row_ref[slot]], NT_DIMS, preferred_element_type=F32)
+
+    acc[...] = second(own, me)
 
     def take_step(j, carry):
         src = lax.rem(me + n - distance(n - 2 - j), n)
@@ -110,7 +117,7 @@
             device_id={"ao": src},
             device_id_type=MESH,
         ).wait_recv()
-        acc[...] += jnp.dot(got[src], coef(src), preferred_element_type=F32)
+        acc[...] += second(got[src], src)
         return carry
 
     lax.fori_loop(0, n - 1, take_step, 0, unroll=n <= 16)
@@ -125,7 +132,7 @@
         ],
         axis=0,
     ).astype(BF16)
-    loads[3].wait()
+    loads[2].wait()
     zeta = jnp.dot(flat, rdm[...], preferred_element_type=F32)
     for t in range(ACT):
         zeta_t[t] = zeta[:, t * ACT : (t + 1) * ACT]
@@ -254,8 +261,9 @@
             ),
             scratch_shapes=[
                 pltpu.VMEM((vec_all, TILE, TILE), BF16),
-                pltpu.VMEM((nao // TILE, TILE, TILE), BF16),
-                pltpu.VMEM((nao // TILE, TILE, norb), BF16),
+                pltpu.VMEM((ACT_ROWS, nao), BF16),
+                pltpu.VMEM((nao // TILE, ACT_ROWS, TILE), BF16),
+                pltpu.VMEM((nao // TILE, norb, TILE), BF16),
                 pltpu.VMEM(rdm_two.shape, BF16),
                 pltpu.VMEM((n, rows, TILE), BF16),
                 pltpu.VMEM((n, rows, TILE), BF16),
@@ -278,7 +286,7 @@
             ),
         )(
             tile_row, tile_col, tile_live, chol_tiles,
-            orbitals.reshape(nao // TILE, TILE, norb), rdm_two,
+            orbitals.T, rdm_two,
         )
         return b.reshape(vec, ACT, norb), q_t.T
 

time: 45.8 us -> 40 us (0.87)
  local copies, waits for them, and re-layouts: 9.53 us -> 3.12 us
  Pallas kernels: 35.4 us -> 36 us
    unnamed x3 -> x2, local copies, waits for them, and re-layouts: 9.53 us -> 3.12 us
    pallas_call x1, Pallas kernels: 35.4 us -> 36 us  [on_device(): pl.pallas_call(functools.partial(kernel, n, vec, norb, per, owners), out_...]
where the time goes in v3:
time: 40 us; the launch traced here: 39.8 us
  Pallas kernels  36 us (90%)
  local copies, waits for them, and re-layouts  3.12 us (8%)
  between operations  0.64 us (2%)
    pallas_call x1, Pallas kernels, on_device(): pl.pallas_call(functools.partial(kernel, n, vec, norb, per, owners), out_...  36 us
    unnamed x2, local copies, waits for them, and re-layouts  3.12 us

profile of v3, /device:TPU:0, one launch (start us, length us, event | category | flops | bytes accessed | tf_op | source)
XLA Modules:
  0.0 39.8 jit_solution(9305309943836383739)
XLA Ops:
  0.6 36.0 %shard_map.77 = (bf16[160,440]{1,0:T(8,128)(2,1)}, f32[40,440]{1,0:T(8,128)}) custom-call(s32[16]{0:T(128)} %row_ref.1, s32[16]{0:T(128)} %col_ref.1, s32[16]{0:T(128)} %live_ref.1, bf16[1,64,128,128]{3,2,1,0:T(8,128)(2,1)} %chol_hbm.1, bf16[440,4096]{1,0:T(8,128)(2,1)} %bitcast.3, bf16[1600,1600]{1,0:T(8,128)(2,1)} %rdm_hbm.1), custom_call_target="tpu_custom_call" | custom-call | tf_op jit(solution)/shard_map/pallas_call | solution.py:250
  36.7 1.6 %copy.10 = bf16[4,40,440]{2,1,0:T(8,128)(2,1)} copy(bf16[4,40,440]{2,1,0:T(8,128)(2,1)} %bitcast.4) | data formatting | bytes 281600
  38.2 1.5 %copy.11 = f32[440,40]{0,1:T(8,128)} copy(f32[440,40]{0,1:T(8,128)} %bitcast.5) | data formatting | bytes 140800

commit v4 on v3

--- a/solution.py
+++ b/solution.py
@@ -17,17 +17,16 @@
 
 
 def kernel(
-    n, vec, norb, per, owners,
+    n, inner, vec, norb, per,
     row_ref, col_ref, live_ref, chol_hbm, orb_hbm, rdm_hbm,
     b_ref, q_ref,
-    chol, act_wide, act, orb, rdm, sent, got, acc, zeta_t, q_parts, q_got, q_sum, q_full,
-    load_sem, send_sem, recv_sem, rs_send, rs_recv, ag_send, ag_recv,
+    chol, act_wide, act, orb, rdm, sent, got, acc, zeta_t,
+    q_parts, q_got, q_line, q_full, b_vmem, q_vmem,
+    load_sem, send_sem, recv_sem, s1_send, s1_recv, s2_send, s2_recv, s3_send, s3_recv,
 ):
     me = lax.axis_index("ao")
     rows = vec * ACT
     flat_len = ACT * ACT
-    lane_blocks = -(-norb // 128)
-    owner_dev = [(o * n) // owners for o in range(owners)]
 
     loads = [
         pltpu.make_async_copy(orb_hbm.at[pl.ds(0, ACT_ROWS)], act_wide, load_sem.at[0]),
@@ -46,7 +45,7 @@
         )
         return carry
 
-    lax.fori_loop(1, n, greet, 0)
+    lax.fori_loop(1, n, greet, 0, unroll=n <= 16)
 
     q_parts[...] = jnp.zeros_like(q_parts)
     live = live_ref[me].astype(F32)
@@ -123,7 +122,9 @@
     lax.fori_loop(0, n - 1, take_step, 0, unroll=n <= 16)
 
     b16 = acc[...].astype(BF16)
-    b_ref[...] = b16
+    b_vmem[...] = b16
+    b_out = pltpu.make_async_copy(b_vmem, b_ref, load_sem.at[0])
+    b_out.start()
     spread = jnp.dot(b16[:, :TILE], pick, preferred_element_type=F32)
     flat = jnp.concatenate(
         [
@@ -146,94 +147,94 @@
         q_t += jnp.dot(high, b_v, preferred_element_type=F32)
         q_t += jnp.dot(low, b_v, preferred_element_type=F32)
 
-    def block_of(k):
-        r, c = k // lane_blocks, k % lane_blocks
-        return r * 8, c * 128, min(128, norb - c * 128)
-
-    blocks = (ACT // 8) * lane_blocks
-    for k in range(blocks):
-        r, c, wide = block_of(k)
+    tiles_of = [
+        (r, c, min(128, norb - c)) for r in range(0, ACT, 8) for c in range(0, norb, 128)
+    ]
+    for k, (r, c, wide) in enumerate(tiles_of):
         q_parts[k // per, k % per, :, pl.ds(0, wide)] = q_t[r : r + 8, c : c + wide]
 
-    def rs_copy(o):
+    plane, spot = me // inner, lax.rem(me, inner)
+    outer = n // inner
+
+    def scatter(e):
+        there = lax.rem(spot + e, inner)
         return pltpu.make_async_remote_copy(
-            src_ref=q_parts.at[o],
-            dst_ref=q_got.at[me],
-            send_sem=rs_send.at[o],
-            recv_sem=rs_recv.at[me],
-            device_id={"ao": owner_dev[o]},
-            device_id_type=MESH,
-        )
-
-    def ag_copy(o, dest):
+            src_ref=q_parts.at[there],
+            dst_ref=q_got.at[e - 1],
+            send_sem=s1_send.at[e - 1],
+            recv_sem=s1_recv.at[e - 1],
+            device_id={"ao": plane * inner + there},
+            device_id_type=MESH,
+        )
+
+    def exchange(e, slot):
         return pltpu.make_async_remote_copy(
-            src_ref=q_sum,
-            dst_ref=q_full.at[o],
-            send_sem=ag_send.at[dest],
-            recv_sem=ag_recv.at[o],
-            device_id={"ao": dest},
-            device_id_type=MESH,
-        )
-
-    for o in range(owners):
-        @pl.when(me != owner_dev[o])
-        def _():
-            rs_copy(o).start()
-
-    for o in range(owners):
-        @pl.when(me == owner_dev[o])
-        def _():
-            q_sum[...] = q_parts[o]
-
-            def add_step(d, carry):
-                src = lax.rem(me + d, n)
-                pltpu.make_async_remote_copy(
-                    src_ref=q_parts.at[o],
-                    dst_ref=q_got.at[src],
-                    send_sem=rs_send.at[o],
-                    recv_sem=rs_recv.at[src],
-                    device_id={"ao": src},
-                    device_id_type=MESH,
-                ).wait_recv()
-                q_sum[...] += q_got[src]
-                return carry
-
-            lax.fori_loop(1, n, add_step, 0)
-
-            def spread_step(d, carry):
-                ag_copy(o, lax.rem(me + d, n)).start()
-                return carry
-
-            lax.fori_loop(1, n, spread_step, 0)
-            q_full[o] = q_sum[...]
-
-    for o in range(owners):
-        @pl.when(me != owner_dev[o])
-        def _():
-            ag_copy(o, owner_dev[o]).wait_recv()
-
-    for k in range(blocks):
-        r, c, wide = block_of(k)
-        q_ref[pl.ds(r, 8), pl.ds(c, wide)] = q_full[k // per, k % per, :, pl.ds(0, wide)]
+            src_ref=q_line.at[slot],
+            dst_ref=q_line.at[slot],
+            send_sem=s2_send.at[e - 1],
+            recv_sem=s2_recv.at[slot],
+            device_id={"ao": lax.rem(plane + e, outer) * inner + spot},
+            device_id_type=MESH,
+        )
+
+    def gather(e, slot):
+        return pltpu.make_async_remote_copy(
+            src_ref=q_full.at[slot],
+            dst_ref=q_full.at[slot],
+            send_sem=s3_send.at[e - 1],
+            recv_sem=s3_recv.at[slot],
+            device_id={"ao": plane * inner + lax.rem(spot + e, inner)},
+            device_id_type=MESH,
+        )
+
+    for e in range(1, inner):
+        scatter(e).start()
+    part = q_parts[spot]
+    for e in range(1, inner):
+        scatter(e).wait_recv()
+        part += q_got[e - 1]
+    q_line[plane] = part
+    for e in range(1, outer):
+        exchange(e, plane).start()
+    for e in range(1, outer):
+        exchange(e, lax.rem(plane + outer - e, outer)).wait_recv()
+    total = q_line[0]
+    for z in range(1, outer):
+        total += q_line[z]
+    q_full[spot] = total
+    for e in range(1, inner):
+        gather(e, spot).start()
+    for e in range(1, inner):
+        gather(e, lax.rem(spot + inner - e, inner)).wait_recv()
+
+    for k, (r, c, wide) in enumerate(tiles_of):
+        q_vmem[pl.ds(r, 8), pl.ds(c, wide)] = q_full[k // per, k % per, :, pl.ds(0, wide)]
+    q_out = pltpu.make_async_copy(q_vmem, q_ref, load_sem.at[1])
+    q_out.start()
 
     def drain(d, carry):
-        dest = lax.rem(me + d, n)
-        slot_copy(dest, me).wait_send()
+        slot_copy(lax.rem(me + d, n), me).wait_send()
         return carry
 
     lax.fori_loop(1, n, drain, 0)
-    for o in range(owners):
-        @pl.when(me != owner_dev[o])
-        def _():
-            rs_copy(o).wait_send()
-
-        @pl.when(me == owner_dev[o])
-        def _():
-            def done(d, carry):
-                ag_copy(o, lax.rem(me + d, n)).wait_send()
-                return carry
-
-            lax.fori_loop(1, n, done, 0)
+    for e in range(1, inner):
+        scatter(e).wait_send()
+        gather(e, spot).wait_send()
+    for e in range(1, outer):
+        exchange(e, plane).wait_send()
+    b_out.wait()
+    q_out.wait()
+
+
+def hand_over(b_in, q_in, b_ref, q_ref, sems):
+    copies = [
+        pltpu.make_async_copy(b_in, b_ref, sems.at[0]),
+        pltpu.make_async_copy(q_in, q_ref, sems.at[1]),
+    ]
+    for copy in copies:
+        copy.start()
+    for copy in copies:
+        copy.wait()
 
 
 def solution(mesh):
@@ -245,20 +246,18 @@
         vec = vec_all // n
         rows = vec * ACT
         blocks = (ACT // 8) * (-(-norb // 128))
-        per = -(-blocks // n)
-        owners = -(-blocks // per)
+        inner = 4 if n % 4 == 0 else 1
+        outer = n // inner
+        per = -(-blocks // inner)
         b, q_t = pl.pallas_call(
-            functools.partial(kernel, n, vec, norb, per, owners),
+            functools.partial(kernel, n, inner, vec, norb, per),
             out_shape=(
                 jax.ShapeDtypeStruct((rows, norb), BF16),
                 jax.ShapeDtypeStruct((ACT, norb), F32),
             ),
             in_specs=[pl.BlockSpec(memory_space=pltpu.SMEM)] * 3
             + [pl.BlockSpec(memory_space=pl.ANY)] * 3,
-            out_specs=(
-                pl.BlockSpec(memory_space=pltpu.VMEM),
-                pl.BlockSpec(memory_space=pltpu.VMEM),
-            ),
+            out_specs=(pl.BlockSpec(memory_space=pl.ANY),) * 2,
             scratch_shapes=[
                 pltpu.VMEM((vec_all, TILE, TILE), BF16),
                 pltpu.VMEM((ACT_ROWS, nao), BF16),
@@ -269,17 +268,21 @@
                 pltpu.VMEM((n, rows, TILE), BF16),
                 pltpu.VMEM((rows, norb), F32),
                 pltpu.VMEM((ACT, vec, ACT), F32),
-                pltpu.VMEM((owners, per, 8, 128), F32),
-                pltpu.VMEM((n, per, 8, 128), F32),
-                pltpu.VMEM((per, 8, 128), F32),
-                pltpu.VMEM((owners, per, 8, 128), F32),
+                pltpu.VMEM((inner, per, 8, 128), F32),
+                pltpu.VMEM((inner, per, 8, 128), F32),
+                pltpu.VMEM((outer, per, 8, 128), F32),
+                pltpu.VMEM((inner, per, 8, 128), F32),
+                pltpu.VMEM((rows, norb), BF16),
+                pltpu.VMEM((ACT, norb), F32),
                 pltpu.SemaphoreType.DMA((4,)),
                 pltpu.SemaphoreType.DMA((n,)),
                 pltpu.SemaphoreType.DMA((n,)),
-                pltpu.SemaphoreType.DMA((owners,)),
-                pltpu.SemaphoreType.DMA((n,)),
-                pltpu.SemaphoreType.DMA((n,)),
-                pltpu.SemaphoreType.DMA((owners,)),
+                pltpu.SemaphoreType.DMA((inner,)),
+                pltpu.SemaphoreType.DMA((inner,)),
+                pltpu.SemaphoreType.DMA((outer,)),
+                pltpu.SemaphoreType.DMA((outer,)),
+                pltpu.SemaphoreType.DMA((inner,)),
+                pltpu.SemaphoreType.DMA((inner,)),
             ],
             compiler_params=pltpu.CompilerParams(
                 collective_id=0, has_side_effects=True, vmem_limit_bytes=56 * 1024 * 1024
@@ -288,6 +291,17 @@
             tile_row, tile_col, tile_live, chol_tiles,
             orbitals.T, rdm_two,
         )
+        b, q_t = pl.pallas_call(
+            hand_over,
+            out_shape=(
+                jax.ShapeDtypeStruct((rows, norb), BF16),
+                jax.ShapeDtypeStruct((ACT, norb), F32),
+            ),
+            in_specs=[pl.BlockSpec(memory_space=pl.ANY)] * 2,
+            out_specs=(pl.BlockSpec(memory_space=pl.ANY),) * 2,
+            scratch_shapes=[pltpu.SemaphoreType.DMA((2,))],
+            compiler_params=pltpu.CompilerParams(vmem_limit_bytes=56 * 1024 * 1024),
+        )(b, q_t)
         return b.reshape(vec, ACT, norb), q_t.T
 
     return jax.shard_map(

time: 40 us -> 46.1 us (1.15)
  Pallas kernels: 36 us -> 45.2 us
  local copies, waits for them, and re-layouts: 3.12 us -> 0 us
    pallas_call x1 -> x2, Pallas kernels: 36 us -> 45.2 us  [the longest x1 36.7 us: on_device(): pl.pallas_call(functools.partial(kernel, n, inner, vec, norb, per), out_s...]
    unnamed x2 -> x0, local copies, waits for them, and re-layouts: 3.12 us -> none
where the time goes in v4:
time: 46.1 us; the launch traced here: 45.9 us
  Pallas kernels  45.2 us (98%)
  between operations  0.64 us (1%)
    pallas_call x1, Pallas kernels, on_device(): pl.pallas_call(functools.partial(kernel, n, inner, vec, norb, per), out_s...  36.7 us
    pallas_call x1, Pallas kernels, on_device(): pl.pallas_call(hand_over, out_shape=(jax.ShapeDtypeStruct((rows, norb), B...  8.57 us

profile of v4, /device:TPU:0, one launch (start us, length us, event | category | flops | bytes accessed | tf_op | source)
XLA Modules:
  0.0 45.9 jit_solution(13258743878221322587)
XLA Ops:
  0.6 36.7 %shard_map.77 = (bf16[160,440]{1,0:T(8,128)(2,1)}, f32[40,440]{1,0:T(8,128)}) custom-call(s32[16]{0:T(128)} %row_ref.1, s32[16]{0:T(128)} %col_ref.1, s32[16]{0:T(128)} %live_ref.1, bf16[1,64,128,128]{3,2,1,0:T(8,128)(2,1)} %chol_hbm.1, bf16[440,4096]{1,0:T(8,128)(2,1)} %bitcast.3, bf16[1600,1600]{1,0:T(8,128)(2,1)} %rdm_hbm.1), custom_call_target="tpu_custom_call" | custom-call | tf_op jit(solution)/shard_map/pallas_call | solution.py:252
  37.3 8.6 %shard_map.78 = (bf16[160,440]{1,0:T(8,128)(2,1)}, f32[40,440]{1,0:T(8,128)}) custom-call(bf16[160,440]{1,0:T(8,128)(2,1)} %get-tuple-element.6.b_in, f32[40,440]{1,0:T(8,128)} %get-tuple-element.7.q_in), custom_call_target="tpu_custom_call" | custom-call | tf_op jit(solution)/shard_map/pallas_call | solution.py:294

commit v5 on v3

--- a/solution.py
+++ b/solution.py
@@ -234,6 +234,11 @@
                 return carry
 
             lax.fori_loop(1, n, done, 0)
+
+
+def hand_over(b_in, q_in, b_ref, q_ref):
+    b_ref[...] = b_in[...]
+    q_ref[...] = q_in[...]
 
 
 def solution(mesh):
@@ -288,6 +293,16 @@
             tile_row, tile_col, tile_live, chol_tiles,
             orbitals.T, rdm_two,
         )
+        b, q_t = pl.pallas_call(
+            hand_over,
+            out_shape=(
+                jax.ShapeDtypeStruct((rows, norb), BF16),
+                jax.ShapeDtypeStruct((ACT, norb), F32),
+            ),
+            in_specs=[pl.BlockSpec(memory_space=pltpu.VMEM)] * 2,
+            out_specs=(pl.BlockSpec(memory_space=pltpu.VMEM),) * 2,
+            compiler_params=pltpu.CompilerParams(vmem_limit_bytes=56 * 1024 * 1024),
+        )(b, q_t)
         return b.reshape(vec, ACT, norb), q_t.T
 
     return jax.shard_map(

time: 40 us -> 38.5 us (0.963)
  local copies, waits for them, and re-layouts: 3.12 us -> 0 us
  Pallas kernels: 36 us -> 37.7 us
    unnamed x2 -> x0, local copies, waits for them, and re-layouts: 3.12 us -> none
    pallas_call x0 -> x1, Pallas kernels: none -> 1.67 us  [on_device(): pl.pallas_call(hand_over, out_shape=(jax.ShapeDtypeStruct((rows, norb), B...]
where the time goes in v5:
time: 38.5 us; the launch traced here: 38.3 us
  Pallas kernels  37.7 us (98%)
  between operations  0.64 us (2%)
    pallas_call x1, Pallas kernels, on_device(): pl.pallas_call(functools.partial(kernel, n, vec, norb, per, owners), out_...  36 us
    pallas_call x1, Pallas kernels, on_device(): pl.pallas_call(hand_over, out_shape=(jax.ShapeDtypeStruct((rows, norb), B...  1.67 us

profile of v5, /device:TPU:0, one launch (start us, length us, event | category | flops | bytes accessed | tf_op | source)
XLA Modules:
  0.0 38.3 jit_solution(5403455158141808332)
XLA Ops:
  0.6 36.0 %shard_map.77 = (bf16[160,440]{1,0:T(8,128)(2,1)}, f32[40,440]{1,0:T(8,128)}) custom-call(s32[16]{0:T(128)} %row_ref.1, s32[16]{0:T(128)} %col_ref.1, s32[16]{0:T(128)} %live_ref.1, bf16[1,64,128,128]{3,2,1,0:T(8,128)(2,1)} %chol_hbm.1, bf16[440,4096]{1,0:T(8,128)(2,1)} %bitcast.3, bf16[1600,1600]{1,0:T(8,128)(2,1)} %rdm_hbm.1), custom_call_target="tpu_custom_call" | custom-call | tf_op jit(solution)/shard_map/pallas_call | solution.py:255
  36.7 1.7 %shard_map.78 = (bf16[160,440]{1,0:T(8,128)(2,1)}, f32[40,440]{1,0:T(8,128)}) custom-call(bf16[160,440]{1,0:T(8,128)(2,1)} %get-tuple-element.6.b_in, f32[40,440]{1,0:T(8,128)} %get-tuple-element.7.q_in), custom_call_target="tpu_custom_call" | custom-call | tf_op jit(solution)/shard_map/pallas_call | solution.py:296

commit v6 on v5

--- a/solution.py
+++ b/solution.py
@@ -77,23 +77,24 @@
             device_id_type=MESH,
         )
 
-    far = lax.rem(me + n // 2, n)
-    sent[far] = half(far)
-    pl.semaphore_wait(barrier, n - 1)
-    slot_copy(far, me).start()
     for k in range(ntiles):
         pltpu.make_async_copy(
             orb_hbm.at[:, pl.ds(k * TILE, TILE)], orb.at[k], load_sem.at[3]
         ).start()
     loads[2].start()
 
-    def send_step(i, carry):
+    def half_step(i, carry):
         dest = lax.rem(me + distance(i), n)
         sent[dest] = half(dest)
-        slot_copy(dest, me).start()
-        return carry
-
-    lax.fori_loop(1, n - 1, send_step, 0, unroll=n <= 16)
+        return carry
+
+    def send_step(i, carry):
+        slot_copy(lax.rem(me + distance(i), n), me).start()
+        return carry
+
+    lax.fori_loop(0, n - 1, half_step, 0, unroll=n <= 16)
+    pl.semaphore_wait(barrier, n - 1)
+    lax.fori_loop(0, n - 1, send_step, 0, unroll=n <= 16)
 
     own = half(me)
     column = lax.broadcasted_iota(jnp.int32, (1, flat_len), 1)

time: 38.5 us -> 38.9 us (1.010)
  Pallas kernels: 37.7 us -> 38.1 us
where the time goes in v6:
time: 38.9 us; the launch traced here: 38.7 us
  Pallas kernels  38.1 us (98%)
  between operations  0.64 us (2%)
    pallas_call x1, Pallas kernels, on_device(): pl.pallas_call(functools.partial(kernel, n, vec, norb, per, owners), out_...  36.4 us
    pallas_call x1, Pallas kernels, on_device(): pl.pallas_call(hand_over, out_shape=(jax.ShapeDtypeStruct((rows, norb), B...  1.67 us

profile of v6, /device:TPU:0, one launch (start us, length us, event | category | flops | bytes accessed | tf_op | source)
XLA Modules:
  0.0 38.7 jit_solution(14866877328963982189)
XLA Ops:
  0.6 36.4 %shard_map.77 = (bf16[160,440]{1,0:T(8,128)(2,1)}, f32[40,440]{1,0:T(8,128)}) custom-call(s32[16]{0:T(128)} %row_ref.1, s32[16]{0:T(128)} %col_ref.1, s32[16]{0:T(128)} %live_ref.1, bf16[1,64,128,128]{3,2,1,0:T(8,128)(2,1)} %chol_hbm.1, bf16[440,4096]{1,0:T(8,128)(2,1)} %bitcast.3, bf16[1600,1600]{1,0:T(8,128)(2,1)} %rdm_hbm.1), custom_call_target="tpu_custom_call" | custom-call | tf_op jit(solution)/shard_map/pallas_call | solution.py:256
  37.0 1.7 %shard_map.78 = (bf16[160,440]{1,0:T(8,128)(2,1)}, f32[40,440]{1,0:T(8,128)}) custom-call(bf16[160,440]{1,0:T(8,128)(2,1)} %get-tuple-element.6.b_in, f32[40,440]{1,0:T(8,128)} %get-tuple-element.7.q_in), custom_call_target="tpu_custom_call" | custom-call | tf_op jit(solution)/shard_map/pallas_call | solution.py:297
